TPU v7x, 128 devices: a whole 4x4x4 slice. The times are simulated.
128 devices in a mesh: ctx: 32 (over z, x, y_hi), head: 4 (over y_lo, core).
Axes of the slice: x: 4, y: 4 (y_hi: 2, y_lo: 2; y = y_hi * 2 + y_lo), z: 4, core: 2. Of those that a mesh axis runs over, the one named last changes fastest.
Arguments:
- probe_vectors: bfloat16 [1024, 8192], P('ctx', 'head'), may hold values from -160 to 160
- lookup_tensor: bfloat16 [32768, 1024], P('ctx', 'head'), may hold values from -4.5 to 4.5
- payload_tensor: bfloat16 [32768, 1024], P('ctx', 'head'), may hold values from -6 to 6
- sequence_locations: int32 [1024], replicated, may hold values from 0 to 32767, as said below
- attention_return_matrix: bfloat16 [8192, 8192], P('head', 'ctx'), may hold values from -0.0625 to 0.0625
- skip_stream_state: bfloat16 [1024, 8192], P('head', 'ctx'), may hold values from -4 to 4
- early_rescaling_factor: float32 [8192], P('ctx'), may hold values from 0.5 to 1.5
- lexicon_projection_matrix: bfloat16 [8192, 65536], P(None, ('ctx', 'head')), may hold values from -0.1875 to 0.1875
- calibrating_divisor: float32 [1024], replicated, may hold values from 0.02 to 1
- desired_tokens_list: int32 [1024], replicated, may hold values from 0 to 65535
Outputs:
- hidden: bfloat16 [1024, 8192], P('head', 'ctx')
- logprob: float32 [1024], replicated
Inputs may be any that keep to these rules, and one draw needn't show every extreme that they name: `sequence_locations`: query i stands at a position from i * 32 to (i + 1) * 32 - 1; the last query stands at 32767.
All inputs are finite; a program needn't handle non-finite values.
Results may differ from a plain program's by a relative error of at most 0.0014.
The roundings to bfloat16 on the way count: a program that leaves them out, or rounds other values in their place, can miss the bound.
Values may be sent and summed in bfloat16 or wider, within the bound.
A program may use at most 192 MiB of HBM per device.

v0:
```python
import math
import jax
import jax.numpy as jnp
from jax import lax
from jax.sharding import Mesh
from jax.sharding import PartitionSpec as P

D = 8192
QUERY_HEAD_COUNT = 64
KEY_VALUE_HEADS = 8
HEAD_SIZE = 128
CTX = ("ctx_0", "ctx_1", "ctx_2")
HEAD = ("head_0", "head_1")
CTX_HEAD = ("ctx_0", "ctx_1", "ctx_2", "head_0", "head_1")
neg_big = -1e30
eps = 1e-05


def copy_for_each(x, axis):
    devices = lax.axis_size(axis)
    return lax.all_to_all(jnp.broadcast_to(x[None], (devices, *x.shape)), axis, 0, 0, tiled=True)


def taken_together(x, axis):
    everything = copy_for_each(x, axis)
    return jnp.max(everything, axis=0)


def sent_together(arrays, axis, dim, along):
    widths = [math.prod(a.shape[along:]) for a in arrays]
    both = jnp.concatenate(
        [a.reshape(*a.shape[:along], w) for a, w in zip(arrays, widths)], axis=along
    )
    result = lax.psum_scatter(both, axis, scatter_dimension=dim, tiled=True)
    tiles = jnp.split(result, [sum(widths[:k]) for k in range(1, len(widths))], axis=along)
    return tuple(
        (b.reshape(*result.shape[:along], *a.shape[along:]) for a, b in zip(arrays, tiles))
    )


def in_blocks(x, dim, devices):
    shape = x.shape
    tiles = x.reshape(*shape[:dim], devices, shape[dim] // devices, *shape[dim + 1 :])
    return jnp.moveaxis(tiles, dim, 0)


def sent_and_summed(x, axis, dim):
    devices = lax.axis_size(axis)
    tiles = lax.all_to_all(in_blocks(x, dim, devices), axis, 0, 0, tiled=True)
    return jnp.sum(tiles, axis=0)


def of_everyone(x, axis):
    everything = copy_for_each(x, axis)
    return jnp.sum(everything, axis=0)


def collected_together(x, axis):
    leaves = jax.tree.leaves(x)
    sequence = sorted(range(len(leaves)), key=lambda k: -leaves[k].size)
    width = (1, *leaves[sequence[0]].shape)[-1]
    lines = [
        jnp.pad(leaves[k].reshape(-1), (0, -leaves[k].size % width)).reshape(-1, width)
        for k in sequence
    ]
    both, at, found = (lax.all_gather(jnp.concatenate(lines), axis), 0, {})
    for k, line in zip(sequence, lines):
        slab = both[:, at : at + len(line)].reshape(len(both), -1)
        found[k] = slab[:, : leaves[k].size].reshape(-1, *leaves[k].shape)
        at += len(line)
    numbers = iter(range(len(leaves)))
    return jax.tree.map(lambda _: found[next(numbers)], x)


def joined_all(x, axes, combine):
    for axis in axes:
        pieces = collected_together(x, axis)
        x = jax.tree.map(lambda part: part[0], pieces)
        for k in range(1, lax.axis_size(axis)):
            x = combine(x, jax.tree.map(lambda part: part[k], pieces))
    return x


def unite_vocab(first, second):
    peak_first, total_first, picked_first = first
    peak_second, total_second, picked_second = second
    joined = jnp.maximum(peak_first, peak_second)
    total = total_first * jnp.exp(peak_first - joined) + total_second * jnp.exp(
        peak_second - joined
    )
    return (joined, total, picked_first + picked_second)


def local_attention(every_query, lookup_tensor, payload_tensor, sequence_locations, key_start):
    total_rows = every_query.shape[0]
    ctx_len = lookup_tensor.shape[0]
    kv_here = lookup_tensor.shape[1] // HEAD_SIZE
    group_size = QUERY_HEAD_COUNT // KEY_VALUE_HEADS
    scale_factor = HEAD_SIZE ** (-0.5)
    row_block = min(512, total_rows)
    query_heads = every_query.reshape(total_rows, kv_here, group_size, HEAD_SIZE)
    key_heads = lookup_tensor.reshape(ctx_len, kv_here, HEAD_SIZE)
    value_heads = payload_tensor.reshape(ctx_len, kv_here, HEAD_SIZE)
    key_pos = key_start + jnp.arange(ctx_len, dtype=jnp.int32)
    maxima, sums, accums = ([], [], [])
    for row_start in range(0, total_rows, row_block):
        row_pos = sequence_locations[row_start : row_start + row_block]
        visible = key_pos[None, None, :] <= row_pos[:, None, None]
        head_max, head_sum, head_acc = ([], [], [])
        for kv_head in range(kv_here):
            scores = (
                jnp.einsum(
                    "qhd,kd->qhk",
                    query_heads[row_start : row_start + row_block, kv_head],
                    key_heads[:, kv_head],
                    preferred_element_type=jnp.float32,
                )
                * scale_factor
            )
            block_max = jnp.max(jnp.where(visible, scores, neg_big), axis=-1)
            weights = jnp.where(visible, jnp.exp(scores - block_max[..., None]), 0.0)
            head_sum.append(jnp.sum(weights, axis=-1))
            head_max.append(block_max)
            head_acc.append(
                jnp.einsum(
                    "qhk,kd->qhd",
                    weights.astype(jnp.bfloat16),
                    value_heads[:, kv_head],
                    preferred_element_type=jnp.float32,
                )
            )
        maxima.append(jnp.concatenate(head_max, axis=1))
        sums.append(jnp.concatenate(head_sum, axis=1))
        accums.append(jnp.concatenate(head_acc, axis=1))
    return (
        jnp.concatenate(maxima, axis=0),
        jnp.concatenate(sums, axis=0),
        jnp.concatenate(accums, axis=0),
    )


def shards(
    probe_vectors,
    lookup_tensor,
    payload_tensor,
    sequence_locations,
    attention_return_matrix,
    skip_stream_state,
    early_rescaling_factor,
    lexicon_projection_matrix,
    calibrating_divisor,
    desired_tokens_list,
):
    heads_here = probe_vectors.shape[1] // HEAD_SIZE
    every_query = lax.all_gather(probe_vectors, CTX, axis=0, tiled=True)
    key_start = lax.axis_index(CTX) * lookup_tensor.shape[0]
    local_max, local_sum, local_acc = local_attention(
        every_query, lookup_tensor, payload_tensor, sequence_locations, key_start
    )
    global_max = taken_together(local_max.astype(jnp.bfloat16), CTX).astype(local_max.dtype)
    rescale = jnp.exp(local_max - global_max)
    acc_rows, sum_rows = sent_together(
        (local_acc * rescale[..., None], local_sum * rescale), CTX, 0, 2
    )
    attn = (
        (acc_rows / sum_rows[..., None])
        .astype(jnp.bfloat16)
        .reshape(acc_rows.shape[0], heads_here * HEAD_SIZE)
    )
    mixed_part = jnp.dot(
        lax.all_gather(attn, CTX, axis=0, tiled=True),
        attention_return_matrix,
        preferred_element_type=jnp.float32,
    )
    mixed_rows = sent_and_summed(mixed_part, HEAD, 0)
    hidden = (skip_stream_state.astype(jnp.float32) + mixed_rows).astype(jnp.bfloat16)
    widened = hidden.astype(jnp.float32)
    square_total = of_everyone(jnp.sum(widened * widened, axis=1), CTX)
    normed = (
        widened * lax.rsqrt(square_total / D + eps)[:, None] * early_rescaling_factor[None, :]
    ).astype(jnp.bfloat16)
    full_rows = lax.all_gather(normed, CTX, axis=1, tiled=True)
    early_class_energies = jnp.dot(
        lax.all_gather(full_rows, HEAD, axis=0, tiled=True),
        lexicon_projection_matrix,
        preferred_element_type=jnp.float32,
    )
    tempered_affinities = early_class_energies / calibrating_divisor[:, None]
    vocab_here = lexicon_projection_matrix.shape[1]
    offset = (lax.axis_index(CTX) * lax.axis_size(HEAD) + lax.axis_index(HEAD)) * vocab_here
    column_ids = jnp.arange(vocab_here, dtype=jnp.int32)[None, :] + offset
    picked = jnp.sum(
        jnp.where(column_ids == desired_tokens_list[:, None], tempered_affinities, 0.0), axis=1
    )
    local_peak = jnp.max(tempered_affinities, axis=1)
    local_total = jnp.sum(jnp.exp(tempered_affinities - local_peak[:, None]), axis=1)
    peak, total, target_logit = joined_all((local_peak, local_total, picked), CTX_HEAD, unite_vocab)
    logprob = target_logit - peak - jnp.log(total)
    return (hidden, logprob)


def solution(mesh):
    torus = Mesh(
        mesh.devices.reshape(4, 4, 2, 2, 2), ("ctx_0", "ctx_1", "ctx_2", "head_0", "head_1")
    )
    placed = (
        P(CTX, HEAD),
        P(CTX, HEAD),
        P(CTX, HEAD),
        P(),
        P(HEAD, CTX),
        P(HEAD, CTX),
        P(CTX),
        P(None, CTX_HEAD),
        P(),
        P(),
    )
    return jax.shard_map(
        shards, mesh=torus, in_specs=placed, out_specs=(P(HEAD, CTX), P()), check_vma=False
    )
```

profile of v0, /device:TPU:1, one launch (start us, length us, event | category | flops | bytes accessed | tf_op | source)
XLA Modules:
  0.0 1000.2 jit_solution(12280744665633798866)
XLA Ops:
  7.2 0.0 copy-start
  7.2 0.0 all-gather.15.cloned.1.call-start
  7.2 0.7 all-gather.15.cloned.1.call-update
  7.9 1.2 copy.117
  9.2 1.2 copy.119
  10.5 0.8 fusion.82
  11.2 0.7 broadcast_compare_fusion.1
  11.9 82.4 %all-gather.15.cloned.1.call-done = bf16[1024,2048]{1,0:T(8,128)(2,1)} async-done(((bf16[32,2048]{1,0:T(8,128)(2,1)}), bf16[1024,2048]{1,0:T(8,128)(2,1)}) %all-gather.15.cloned.1.call-update) | async-done | bytes 4194320 | tf_op jit(solution)/shard_map/all_gather | solution.py:155
  94.2 6.4 copy.115
  100.6 8.8 select_reduce_fusion.3
  109.4 0.0 copy-done.3
  109.4 15.3 %fusion = (f32[512,8]{0,1:T(8,128)S(1)}, f32[512,8]{0,1:T(8,128)S(1)}, f32[512,8,1024]{2,0,1:T(8,128)}) fusion(f32[512,8,1024]{2,0,1:T(8,128)} %get-tuple-element.31, f32[512,8]{0,1:T(8,128)S(1)} %get-tuple-element.30, pred[512,1024]{1,0:T(8,128)(4,1)S(1)} %get-tuple-element.23, bf16[1024,2,128]{0,2,1:T(8,128)(2,1)S(1)} %bitcast.321, ...), kind=kOutput, calls=%fused_computation.9 | convolution fusion | flops 1103093760 | bytes 35438592 | tf_op jit(solution)/shard_map/qhd,kd->qhk/dot_general | solution.py:112
  124.7 8.5 fusion.14
  133.1 7.4 select_reduce_fusion.1
  140.6 8.5 fusion.10
  149.0 15.3 %fusion.4 = (f32[512,8]{0,1:T(8,128)S(1)}, f32[512,8]{0,1:T(8,128)S(1)}, f32[512,8,1024]{2,0,1:T(8,128)}) fusion(f32[512,8,1024]{2,0,1:T(8,128)} %get-tuple-element.28, f32[512,8]{0,1:T(8,128)S(1)} %get-tuple-element.27, pred[512,1024]{1,0:T(8,128)(4,1)S(1)} %get-tuple-element.24, bf16[1024,2,128]{0,2,1:T(8,128)(2,1)S(1)} %bitcast.323, ...), kind=kOutput, calls=%fused_computation.13 | convolution fusion | flops 1103093760 | bytes 35438592 | tf_op jit(solution)/shard_map/qhd,kd->qhk/dot_general | solution.py:112
  164.3 8.8 fusion.12
  173.1 2.5 copy-done.2
  175.6 11.1 %fusion.2 = (f32[512,8]{0,1:T(8,128)S(1)}, f32[512,8]{0,1:T(8,128)S(1)}) fusion(f32[512,8,1024]{2,0,1:T(8,128)} %get-tuple-element.32, f32[512,8]{0,1:T(8,128)S(1)} %get-tuple-element.5, pred[512,1024]{1,0:T(8,128)(4,1)S(1)} %get-tuple-element.23, f32[512,8]{0,1:T(8,128)S(1)} %get-tuple-element.7, f32[512,8,1024]{2,0,1:T(8,128)S(1)} %copy-done.2, ...), kind=kLoop, calls=%fused_computation.11 | loop fusion | flops 33546240 | bytes 34668544 | tf_op jit(solution)/shard_map/reduce_sum | solution.py:122
  186.7 1.1 broadcast_in_dim.79
  187.8 5.3 all-to-all-start
  193.1 0.0 reduce-scatter.2.cloned.1.call-start
  193.1 8.5 fusion.8
  201.6 9.5 all-to-all-done
  211.1 0.2 reduce_max.58
  211.3 4.7 copy.126
  216.0 6.4 maximum_multiply_fusion
  222.5 0.0 copy-done.1
  222.5 6.1 pad_maximum_fusion
  228.5 0.0 reduce-scatter.2.cloned.1.call-update
  228.6 0.0 all-gather.17.cloned.1.call-start
  228.6 357.1 %reduce-scatter.2.cloned.1.call-done = f32[32,16,129]{2,0,1:T(8,128)} async-done(((f32[1024,16,129]{2,0,1:T(8,128)}), f32[32,16,129]{2,0,1:T(8,128)}) %reduce-scatter.2.cloned.1.call-update) | async-done | bytes 264208 | tf_op jit(solution)/shard_map/reduce_scatter | solution.py:34
  585.7 1.1 slice_reduce_fusion
  586.8 1.7 copy_bitcast_fusion
  588.6 0.0 all-gather.17.cloned.1.call-update
  588.6 0.0 all-gather.19.cloned.1.call-start
  588.7 84.5 %all-gather.17.cloned.1.call-done = bf16[1024,2048]{1,0:T(8,128)(2,1)} async-done(((bf16[32,2048]{1,0:T(8,128)(2,1)}), bf16[1024,2048]{1,0:T(8,128)(2,1)}) %all-gather.17.cloned.1.call-update) | async-done | bytes 4194320 | tf_op jit(solution)/shard_map/all_gather | solution.py:171
  673.2 0.0 copy-done
  673.2 3.4 fusion.84
  676.6 16.9 %all_to_all.16 = f32[4,256,256]{2,1,0:T(8,128)S(1)} all-to-all(f32[4,256,256]{2,1,0:T(8,128)S(1)} %bitcast.315), channel_id=1, replica_groups=mesh['ctx_0'=4,'ctx_1'=4,'ctx_2'=2,'head_0'=2,'head_1'=2] {'head_0','hea..., dimensions={0} | all-to-all | bytes 2097152 | tf_op jit(solution)/shard_map/all_to_all | solution.py:49
  693.5 0.1 reduce_sum.85
  693.6 0.0 copy-done.5
  693.6 0.1 fusion.24
  693.8 14.4 %all_to_all.17 = f32[32,1,256]{2,1,0:T(1,128)S(1)} all-to-all(f32[32,1,256]{2,1,0:T(1,128)S(1)} %broadcast_in_dim.80), channel_id=1, replica_groups=mesh['ctx_0'=4,'ctx_1'=4,'ctx_2'=2,'head_0'=2,'head_1'=2] {'ctx_0','ctx_..., dimensions={0} | all-to-all | bytes 65536 | tf_op jit(solution)/shard_map/all_to_all | solution.py:21
  708.2 0.1 reduce_sum.87
  708.2 0.7 fusion.26
  709.0 0.0 all-gather.19.cloned.1.call-update
  709.0 0.0 all-gather.21.cloned.1.call-start
  709.0 77.2 %all-gather.19.cloned.1.call-done = bf16[256,8192]{1,0:T(8,128)(2,1)} async-done(((bf16[256,256]{1,0:T(8,128)(2,1)}), bf16[256,8192]{1,0:T(8,128)(2,1)}) %all-gather.19.cloned.1.call-update) | async-done | bytes 4194320 | tf_op jit(solution)/shard_map/all_gather | solution.py:182
  786.2 0.0 all-gather.21.cloned.1.call-update
  786.3 0.0 copy-start.6
  786.3 153.9 %all-gather.21.cloned.1.call-done = bf16[1024,8192]{1,0:T(8,128)(2,1)} async-done(((bf16[256,8192]{1,0:T(8,128)(2,1)}), bf16[1024,8192]{1,0:T(8,128)(2,1)}) %all-gather.21.cloned.1.call-update) | async-done | bytes 16777232 | tf_op jit(solution)/shard_map/all_gather | solution.py:184
  940.2 17.1 %fusion.83 = (f32[1024]{0:T(1024)S(1)}, f32[1024,512]{0,1:T(8,128)S(1)}) fusion(f32[1024]{0:T(1024)S(1)} %copy-done.8, bf16[1024,8192]{1,0:T(8,128)(2,1)} %all-gather.21.cloned.1.call-done, bf16[8192,512]{1,0:T(8,128)(2,1)} %param.17), kind=kOutput, calls=%fused_computation.154 | convolution fusion | flops 8590982144 | bytes 27271168 | tf_op jit(solution)/shard_map/dot_general | solution.py:183
  957.3 0.0 copy-done.4
  957.3 0.0 copy-done.6
  957.3 0.5 exponential_reduce_fusion
  957.8 9.7 all-gather.5
  967.5 0.1 fusion.54
  967.6 9.3 all-gather.6
  976.9 0.1 fusion.44
  977.0 4.8 all-gather.7
  981.8 3.3 all-gather.8
  985.1 7.9 all-gather.9
  993.1 0.6 log_subtract_fusion
  (31 shorter events, 0.3 us)
Async XLA Ops:
  7.2 666.0 %copy-start = (bf16[2048,256]{1,0:T(8,128)(2,1)S(1)}, bf16[2048,256]{1,0:T(8,128)(2,1)}, u32[]{:S(2)}) copy-start(bf16[2048,256]{1,0:T(8,128)(2,1)} %param.14) | copy-start | bytes 3145732
  7.2 87.1 %all-gather.15.cloned.1.call-start = ((), (), s32[]{:S(2)}) async-start(), calls=%async_computation.4 | async-start | bytes 4325376 | tf_op jit(solution)/shard_map/all_gather | solution.py:155
  100.6 8.8 copy-start.3
  164.3 11.3 %copy-start.2 = (f32[512,8,1024]{2,0,1:T(8,128)S(1)}, f32[512,8,1024]{2,0,1:T(8,128)}, u32[]{:S(2)}) copy-start(f32[512,8,1024]{2,0,1:T(8,128)} %get-tuple-element.29) | copy-start | bytes 50331652
  187.8 23.3 %all-to-all-start = ((bf16[32,1024,16]{1,2,0:T(8,128)(2,1)}), bf16[32,1024,16]{1,2,0:T(8,128)(2,1)S(1)}, u32[]{:S(2)}, u32[]{:S(2)}) async-start(bf16[32,1024,16]{1,2,0:T(8,128)(2,1)} %broadcast_in_dim.79), calls=%async_computation | async-start | bytes 2097152 | tf_op jit(solution)/shard_map/all_to_all | solution.py:21
  193.1 392.7 %reduce-scatter.2.cloned.1.call-start = ((), (), s32[]{:S(2)}) async-start(), calls=%async_computation.5 | async-start | bytes 17301504 | tf_op jit(solution)/shard_map/reduce_scatter | solution.py:34
  216.0 6.4 copy-start.1
  228.5 465.1 %copy-start.5 = (bf16[256,256]{1,0:T(8,128)(2,1)S(1)}, bf16[256,256]{1,0:T(8,128)(2,1)}, u32[]{:S(2)}) copy-start(bf16[256,256]{1,0:T(8,128)(2,1)} %param.15) | copy-start | bytes 393220
  228.5 479.7 %copy-start.7 = (f32[256]{0:T(256)S(1)}, f32[256]{0:T(256)}, u32[]{:S(2)}) copy-start(f32[256]{0:T(256)} %param.16) | copy-start | bytes 3076
  228.5 711.7 %copy-start.8 = (f32[1024]{0:T(1024)S(1)}, f32[1024]{0:T(1024)}, u32[]{:S(2)}) copy-start(f32[1024]{0:T(1024)} %param.18) | copy-start | bytes 12292
  228.6 444.6 %all-gather.17.cloned.1.call-start = ((), (), s32[]{:S(2)}) async-start(), calls=%async_computation.6 | async-start | bytes 4325376 | tf_op jit(solution)/shard_map/all_gather | solution.py:171
  588.6 197.6 %all-gather.19.cloned.1.call-start = ((), (), s32[]{:S(2)}) async-start(), calls=%async_computation.7 | async-start | bytes 4325376 | tf_op jit(solution)/shard_map/all_gather | solution.py:182
  693.7 263.5 %copy-start.4 = (bf16[256,256]{1,0:T(8,128)(2,1)}, bf16[256,256]{1,0:T(8,128)(2,1)S(1)}, u32[]{:S(2)}) copy-start(bf16[256,256]{1,0:T(8,128)(2,1)S(1)} %get-tuple-element.17) | copy-start | bytes 393220
  709.0 231.2 %all-gather.21.cloned.1.call-start = ((), (), s32[]{:S(2)}) async-start(), calls=%async_computation.8 | async-start | bytes 20971520 | tf_op jit(solution)/shard_map/all_gather | solution.py:184
  786.3 171.0 %copy-start.6 = (s32[1024]{0:T(1024)S(1)}, s32[1024]{0:T(1024)}, u32[]{:S(2)}) copy-start(s32[1024]{0:T(1024)} %param.19) | copy-start | bytes 12292
Sparse Core Ops, SparseCore 0:
  11.1 83.0 all-gather.14
  228.7 357.0 reduce-scatter.1
  589.4 83.7 all-gather.16
  709.1 77.0 all-gather.18
  787.7 152.3 all-gather.20
where the time goes:
time: 1000 us
  waiting for transfers between devices  765 us (76%)
  matrix products  101 us (10%)
  blocking collectives  66.2 us (7%)
  other arithmetic  28.6 us (3%)
  local copies, waits for them, and re-layouts  19.1 us (2%)
  between operations  14.1 us (1%)
    reduce_scatter x1, waiting for transfers between devices, sent_together(): result = lax.psum_scatter(both, axis, scatter_dimension=dim, tiled=True)  357 us
    all_gather x1, waiting for transfers between devices, shards(): lax.all_gather(full_rows, HEAD, axis=0, tiled=True)  154 us
    all_gather x1, waiting for transfers between devices, shards(): lax.all_gather(attn, CTX, axis=0, tiled=True)  84.5 us
    all_gather x1, waiting for transfers between devices, shards(): every_query = lax.all_gather(probe_vectors, CTX, axis=0, tiled=True)  82.4 us
    all_gather x1, waiting for transfers between devices, shards(): full_rows = lax.all_gather(normed, CTX, axis=1, tiled=True)  77.2 us
    dot_general x4, matrix products, local_attention(): jnp.einsum('qhd,kd->qhk', query_heads[row_start:row_start + row_block, kv...  46.7 us
    all_gather x5, blocking collectives, collected_together(): both, at, found = (lax.all_gather(jnp.concatenate(lines), axis), 0, {})  34.9 us
    dot_general x4, matrix products, local_attention(): jnp.einsum('qhk,kd->qhd', weights.astype(jnp.bfloat16), value_heads[:, kv...  34.2 us
  transfers between devices with their start and end apart: 6, of which 6 were waited for; matrix products, arithmetic and copies ran while one was open for 1% of the time, Pallas kernels for 0%

commit v1 on v0

--- a/solution.py
+++ b/solution.py
@@ -180,8 +180,11 @@
         widened * lax.rsqrt(square_total / D + eps)[:, None] * early_rescaling_factor[None, :]
     ).astype(jnp.bfloat16)
     full_rows = lax.all_gather(normed, CTX, axis=1, tiled=True)
+    compute_domain = lambda buf, axis_tag: jnp.concatenate(
+        lax.all_to_all(jnp.stack(lax.axis_size(axis_tag) * [buf], 0), axis_tag, 0, 0), 0
+    )
     early_class_energies = jnp.dot(
-        lax.all_gather(full_rows, HEAD, axis=0, tiled=True),
+        compute_domain(full_rows, axis_tag=HEAD),
         lexicon_projection_matrix,
         preferred_element_type=jnp.float32,
     )

time: 1000 us -> 1050 us (1.050)
  waiting for transfers between devices: 765 us -> 794 us
    all_to_all x0 -> x1, waiting for transfers between devices: none -> 182 us  [shards(): lax.all_to_all(jnp.stack(lax.axis_size(axis_tag) * [buf], 0), axis_tag, 0...]
    all_gather x1 -> x0, waiting for transfers between devices: 154 us -> none  [shards(): lax.all_gather(full_rows, HEAD, axis=0, tiled=True)]
where the time goes in v1:
time: 1050 us
  waiting for transfers between devices  794 us (76%)
  matrix products  101 us (10%)
  blocking collectives  68 us (6%)
  other arithmetic  28.6 us (3%)
  local copies, waits for them, and re-layouts  26.5 us (3%)
  between operations  14.1 us (1%)
  starting transfers between devices  13.6 us (1%)
    reduce_scatter x1, waiting for transfers between devices, sent_together(): result = lax.psum_scatter(both, axis, scatter_dimension=dim, tiled=True)  357 us
    all_to_all x1, waiting for transfers between devices, shards(): lax.all_to_all(jnp.stack(lax.axis_size(axis_tag) * [buf], 0), axis_tag, 0...  182 us
    all_gather x1, waiting for transfers between devices, shards(): lax.all_gather(attn, CTX, axis=0, tiled=True)  84.5 us
    all_gather x1, waiting for transfers between devices, shards(): every_query = lax.all_gather(probe_vectors, CTX, axis=0, tiled=True)  82.4 us
    all_gather x1, waiting for transfers between devices, shards(): full_rows = lax.all_gather(normed, CTX, axis=1, tiled=True)  77.2 us
    dot_general x4, matrix products, local_attention(): jnp.einsum('qhd,kd->qhk', query_heads[row_start:row_start + row_block, kv...  46.7 us
    all_gather x5, blocking collectives, collected_together(): both, at, found = (lax.all_gather(jnp.concatenate(lines), axis), 0, {})  36.7 us
    dot_general x4, matrix products, local_attention(): jnp.einsum('qhk,kd->qhd', weights.astype(jnp.bfloat16), value_heads[:, kv...  34.2 us
  transfers between devices with their start and end apart: 6, of which 6 were waited for; matrix products, arithmetic and copies ran while one was open for 1% of the time, Pallas kernels for 0%

profile of v1, /device:TPU:1, one launch (start us, length us, event | category | flops | bytes accessed | tf_op | source)
XLA Modules:
  0.0 1045.9 jit_solution(4295486074697829829)
XLA Ops:
  7.2 0.0 copy-start
  7.2 0.0 all-gather.14.cloned.1.call-start
  7.2 0.7 all-gather.14.cloned.1.call-update
  7.9 1.2 copy.117
  9.2 1.2 copy.119
  10.5 0.8 fusion.82
  11.2 0.7 broadcast_compare_fusion.1
  11.9 82.4 %all-gather.14.cloned.1.call-done = bf16[1024,2048]{1,0:T(8,128)(2,1)} async-done(((bf16[32,2048]{1,0:T(8,128)(2,1)}), bf16[1024,2048]{1,0:T(8,128)(2,1)}) %all-gather.14.cloned.1.call-update) | async-done | bytes 4194320 | tf_op jit(solution)/shard_map/all_gather | solution.py:155
  94.2 6.4 copy.115
  100.6 8.8 select_reduce_fusion.3
  109.4 0.0 copy-done.3
  109.4 15.3 %fusion = (f32[512,8]{0,1:T(8,128)S(1)}, f32[512,8]{0,1:T(8,128)S(1)}, f32[512,8,1024]{2,0,1:T(8,128)}) fusion(f32[512,8,1024]{2,0,1:T(8,128)} %get-tuple-element.31, f32[512,8]{0,1:T(8,128)S(1)} %get-tuple-element.30, pred[512,1024]{1,0:T(8,128)(4,1)S(1)} %get-tuple-element.23, bf16[1024,2,128]{0,2,1:T(8,128)(2,1)S(1)} %bitcast.322, ...), kind=kOutput, calls=%fused_computation.9 | convolution fusion | flops 1103093760 | bytes 35438592 | tf_op jit(solution)/shard_map/qhd,kd->qhk/dot_general | solution.py:112
  124.7 8.5 fusion.14
  133.1 7.4 select_reduce_fusion.1
  140.6 8.5 fusion.10
  149.0 15.3 %fusion.4 = (f32[512,8]{0,1:T(8,128)S(1)}, f32[512,8]{0,1:T(8,128)S(1)}, f32[512,8,1024]{2,0,1:T(8,128)}) fusion(f32[512,8,1024]{2,0,1:T(8,128)} %get-tuple-element.28, f32[512,8]{0,1:T(8,128)S(1)} %get-tuple-element.27, pred[512,1024]{1,0:T(8,128)(4,1)S(1)} %get-tuple-element.24, bf16[1024,2,128]{0,2,1:T(8,128)(2,1)S(1)} %bitcast.324, ...), kind=kOutput, calls=%fused_computation.13 | convolution fusion | flops 1103093760 | bytes 35438592 | tf_op jit(solution)/shard_map/qhd,kd->qhk/dot_general | solution.py:112
  164.3 8.8 fusion.12
  173.1 2.5 copy-done.2
  175.6 11.1 %fusion.2 = (f32[512,8]{0,1:T(8,128)S(1)}, f32[512,8]{0,1:T(8,128)S(1)}) fusion(f32[512,8,1024]{2,0,1:T(8,128)} %get-tuple-element.32, f32[512,8]{0,1:T(8,128)S(1)} %get-tuple-element.5, pred[512,1024]{1,0:T(8,128)(4,1)S(1)} %get-tuple-element.23, f32[512,8]{0,1:T(8,128)S(1)} %get-tuple-element.7, f32[512,8,1024]{2,0,1:T(8,128)S(1)} %copy-done.2, ...), kind=kLoop, calls=%fused_computation.11 | loop fusion | flops 33546240 | bytes 34668544 | tf_op jit(solution)/shard_map/reduce_sum | solution.py:122
  186.7 1.1 broadcast_in_dim.79
  187.8 5.3 all-to-all-start
  193.1 0.0 reduce-scatter.2.cloned.1.call-start
  193.1 8.5 fusion.8
  201.6 9.5 all-to-all-done
  211.1 0.2 reduce_max.58
  211.3 4.7 copy.126
  216.0 6.4 maximum_multiply_fusion
  222.5 0.0 copy-done.1
  222.5 6.1 pad_maximum_fusion
  228.5 0.0 reduce-scatter.2.cloned.1.call-update
  228.6 0.0 all-gather.16.cloned.1.call-start
  228.6 357.1 %reduce-scatter.2.cloned.1.call-done = f32[32,16,129]{2,0,1:T(8,128)} async-done(((f32[1024,16,129]{2,0,1:T(8,128)}), f32[32,16,129]{2,0,1:T(8,128)}) %reduce-scatter.2.cloned.1.call-update) | async-done | bytes 264208 | tf_op jit(solution)/shard_map/reduce_scatter | solution.py:34
  585.7 1.1 slice_reduce_fusion
  586.8 1.7 copy_bitcast_fusion
  588.6 0.0 all-gather.16.cloned.1.call-update
  588.6 0.0 all-gather.18.cloned.1.call-start
  588.7 84.5 %all-gather.16.cloned.1.call-done = bf16[1024,2048]{1,0:T(8,128)(2,1)} async-done(((bf16[32,2048]{1,0:T(8,128)(2,1)}), bf16[1024,2048]{1,0:T(8,128)(2,1)}) %all-gather.16.cloned.1.call-update) | async-done | bytes 4194320 | tf_op jit(solution)/shard_map/all_gather | solution.py:171
  673.2 0.0 copy-done
  673.2 3.4 fusion.84
  676.6 16.9 %all_to_all.21 = f32[4,256,256]{2,1,0:T(8,128)S(1)} all-to-all(f32[4,256,256]{2,1,0:T(8,128)S(1)} %bitcast.316), channel_id=1, replica_groups=mesh['ctx_0'=4,'ctx_1'=4,'ctx_2'=2,'head_0'=2,'head_1'=2] {'head_0','hea..., dimensions={0} | all-to-all | bytes 2097152 | tf_op jit(solution)/shard_map/all_to_all | solution.py:49
  693.5 0.1 reduce_sum.85
  693.6 0.0 copy-done.5
  693.6 0.1 fusion.24
  693.7 0.0 copy-start.4
  693.8 14.4 %all_to_all.22 = f32[32,1,256]{2,1,0:T(1,128)S(1)} all-to-all(f32[32,1,256]{2,1,0:T(1,128)S(1)} %broadcast_in_dim.80), channel_id=1, replica_groups=mesh['ctx_0'=4,'ctx_1'=4,'ctx_2'=2,'head_0'=2,'head_1'=2] {'ctx_0','ctx_..., dimensions={0} | all-to-all | bytes 65536 | tf_op jit(solution)/shard_map/all_to_all | solution.py:21
  708.1 0.1 reduce_sum.87
  708.2 0.0 copy-done.7
  708.2 0.7 fusion.26
  709.0 0.0 all-gather.18.cloned.1.call-update
  709.0 77.2 %all-gather.18.cloned.1.call-done = bf16[256,8192]{1,0:T(8,128)(2,1)} async-done(((bf16[256,256]{1,0:T(8,128)(2,1)}), bf16[256,8192]{1,0:T(8,128)(2,1)}) %all-gather.18.cloned.1.call-update) | async-done | bytes 4194320 | tf_op jit(solution)/shard_map/all_gather | solution.py:182
  786.2 7.4 stack.2
  793.6 0.0 copy-done.4
  793.6 8.1 all-to-all-start.3
  801.8 182.2 %all-to-all-done.3 = bf16[4,256,8192]{2,1,0:T(8,128)(2,1)} async-done(((bf16[4,256,8192]{2,1,0:T(8,128)(2,1)}), bf16[4,256,8192]{2,1,0:T(8,128)(2,1)}, u32[]{:S(2)}, u32[]{:S(2)}) %all-to-all-start.3) | async-done | bytes 16777248 | tf_op jit(solution)/shard_map/all_to_all | solution.py:184
  984.0 17.1 %fusion.83 = (f32[1024]{0:T(1024)S(1)}, f32[1024,512]{0,1:T(8,128)S(1)}) fusion(f32[1024]{0:T(1024)S(1)} %copy-done.8, bf16[1024,8192]{1,0:T(8,128)(2,1)} %bitcast.21, bf16[8192,512]{1,0:T(8,128)(2,1)} %param.17), kind=kOutput, calls=%fused_computation.154 | convolution fusion | flops 8590982144 | bytes 27271168 | tf_op jit(solution)/shard_map/dot_general | solution.py:186
  1001.1 0.5 exponential_reduce_fusion
  1001.6 9.1 all-gather.5
  1010.8 0.1 fusion.54
  1010.9 9.3 all-gather.6
  1020.2 0.1 fusion.44
  1020.3 4.8 all-gather.7
  1025.1 3.3 all-gather.8
  1028.4 10.3 all-gather.9
  1038.7 0.6 log_subtract_fusion
  (31 shorter events, 0.3 us)
Async XLA Ops:
  7.2 666.0 %copy-start = (bf16[2048,256]{1,0:T(8,128)(2,1)S(1)}, bf16[2048,256]{1,0:T(8,128)(2,1)}, u32[]{:S(2)}) copy-start(bf16[2048,256]{1,0:T(8,128)(2,1)} %param.14) | copy-start | bytes 3145732
  7.2 87.1 %all-gather.14.cloned.1.call-start = ((), (), s32[]{:S(2)}) async-start(), calls=%async_computation.5 | async-start | bytes 4325376 | tf_op jit(solution)/shard_map/all_gather | solution.py:155
  100.6 8.8 copy-start.3
  164.3 11.3 %copy-start.2 = (f32[512,8,1024]{2,0,1:T(8,128)S(1)}, f32[512,8,1024]{2,0,1:T(8,128)}, u32[]{:S(2)}) copy-start(f32[512,8,1024]{2,0,1:T(8,128)} %get-tuple-element.29) | copy-start | bytes 50331652
  187.8 23.3 %all-to-all-start = ((bf16[32,1024,16]{1,2,0:T(8,128)(2,1)}), bf16[32,1024,16]{1,2,0:T(8,128)(2,1)S(1)}, u32[]{:S(2)}, u32[]{:S(2)}) async-start(bf16[32,1024,16]{1,2,0:T(8,128)(2,1)} %broadcast_in_dim.79), calls=%async_computation | async-start | bytes 2097152 | tf_op jit(solution)/shard_map/all_to_all | solution.py:21
  193.1 392.7 %reduce-scatter.2.cloned.1.call-start = ((), (), s32[]{:S(2)}) async-start(), calls=%async_computation.6 | async-start | bytes 17301504 | tf_op jit(solution)/shard_map/reduce_scatter | solution.py:34
  216.0 6.4 copy-start.1
  228.5 465.1 %copy-start.5 = (bf16[256,256]{1,0:T(8,128)(2,1)S(1)}, bf16[256,256]{1,0:T(8,128)(2,1)}, u32[]{:S(2)}) copy-start(bf16[256,256]{1,0:T(8,128)(2,1)} %param.15) | copy-start | bytes 393220
  228.5 479.7 %copy-start.7 = (f32[256]{0:T(256)S(1)}, f32[256]{0:T(256)}, u32[]{:S(2)}) copy-start(f32[256]{0:T(256)} %param.16) | copy-start | bytes 3076
  228.6 444.6 %all-gather.16.cloned.1.call-start = ((), (), s32[]{:S(2)}) async-start(), calls=%async_computation.7 | async-start | bytes 4325376 | tf_op jit(solution)/shard_map/all_gather | solution.py:171
  588.6 197.6 %all-gather.18.cloned.1.call-start = ((), (), s32[]{:S(2)}) async-start(), calls=%async_computation.8 | async-start | bytes 4325376 | tf_op jit(solution)/shard_map/all_gather | solution.py:182
  693.7 99.9 %copy-start.4 = (bf16[256,256]{1,0:T(8,128)(2,1)}, bf16[256,256]{1,0:T(8,128)(2,1)S(1)}, u32[]{:S(2)}) copy-start(bf16[256,256]{1,0:T(8,128)(2,1)S(1)} %get-tuple-element.17) | copy-start | bytes 393220
  793.6 190.4 %copy-start.8 = (f32[1024]{0:T(1024)S(1)}, f32[1024]{0:T(1024)}, u32[]{:S(2)}) copy-start(f32[1024]{0:T(1024)} %param.18) | copy-start | bytes 12292
  793.6 190.4 %all-to-all-start.3 = ((bf16[4,256,8192]{2,1,0:T(8,128)(2,1)}), bf16[4,256,8192]{2,1,0:T(8,128)(2,1)}, u32[]{:S(2)}, u32[]{:S(2)}) async-start(bf16[4,256,8192]{2,1,0:T(8,128)(2,1)} %stack.2), calls=%async_computation.4 | async-start | bytes 33554432 | tf_op jit(solution)/shard_map/all_to_all | solution.py:184
  984.0 17.1 %copy-start.6 = (s32[1024]{0:T(1024)S(1)}, s32[1024]{0:T(1024)}, u32[]{:S(2)}) copy-start(s32[1024]{0:T(1024)} %param.19) | copy-start | bytes 12292
Sparse Core Ops, SparseCore 0:
  11.1 83.0 all-gather.13
  228.7 357.0 reduce-scatter.1
  589.4 83.7 all-gather.15
  709.1 77.0 all-gather.17
